TPU v7x, 256 devices: a whole 4x4x8 slice. The times are simulated.
256 devices in a mesh: seq: 32 (over y, x, core), tp: 8 (over z).
Axes of the slice: x: 4, y: 4, z: 8, core: 2. Of those that a mesh axis runs over, the one named last changes fastest.
Arguments:
- token_ids: int32 [2, 2, 8], replicated, may hold values from 0 to 65535
- lengths: int32 [2], replicated, may hold values from 1 to 131072, as said below
- norm_gain: bfloat16 [8192], P('seq'), may hold values from 0.099609375 to 1.8984375
- emb_table: bfloat16 [65536, 8192], P(('seq', 'tp')), may hold values from -6 to 6
- q_weight: bfloat16 [8192, 8192], P('seq', 'tp'), may hold values from -0.0625 to 0.0625
- key_matrix: bfloat16 [8192, 1024], P('seq', 'tp'), may hold values from -0.26367188 to 0.26367188
- value_matrix: bfloat16 [8192, 1024], P('seq', 'tp'), may hold values from -0.0625 to 0.0625
- o_weight: bfloat16 [8192, 8192], P('tp', 'seq'), may hold values from -0.0625 to 0.0625
- key_cache: bfloat16 [2, 131072, 8, 128], P(None, 'seq', 'tp'), may hold values from -160 to 160
- value_cache: bfloat16 [2, 131072, 8, 128], P(None, 'seq', 'tp'), may hold values from -12 to 12
Outputs:
- attention_out: bfloat16 [32, 8192], P('tp', 'seq')
Inputs may be any that keep to these rules, and one draw needn't show every extreme that they name: `lengths`: every game's history has at least one position; at least one game's history fills all 131072 cache positions.
All inputs are finite; a program needn't handle non-finite values.
Results may differ from a plain program's by a relative error of at most 0.019.
The roundings to bfloat16 on the way count: a program that leaves them out, or rounds other values in their place, can miss the bound.
Values may be sent and summed in bfloat16 or wider, within the bound.
A program may use at most 64 MiB of HBM per device.

v0:
```python
import jax
import jax.numpy as jnp
import numpy as np
from jax import lax
from jax.sharding import PartitionSpec as P

MODEL_WIDTH = 8192
QUERY_HEADS = 64
KEY_HEADS = 8
HEAD_SIZE = 128
GAME_COUNT = 2
CANDIDATE_MOVES = 8
NEW_TOKENS = 2


EPSILON = 1e-05
FLOOR = -1e30


def merged(part, axis, combine):
    gathered = jax.tree.map(lambda a: lax.all_gather(a, axis), part)

    def take(source):
        return jax.tree.map(lambda a: lax.dynamic_index_in_dim(a, source, 0, False), gathered)

    return lax.fori_loop(
        1, lax.axis_size(axis), lambda source, state: combine(state, take(source)), take(0)
    )


def rotary_rates(head_dim):
    half_dim = head_dim // 2
    plain_rate = 500000.0 ** (-(np.arange(half_dim) * 2.0) / head_dim)
    wave_len = 2.0 * np.pi / plain_rate
    blend = (8192.0 / wave_len - 1.0) / 3.0
    scaled = np.where(
        wave_len < 2048.0,
        plain_rate,
        np.where(
            wave_len > 8192.0,
            plain_rate / 8.0,
            (1.0 - blend) * plain_rate / 8.0 + blend * plain_rate,
        ),
    )
    return jnp.asarray(scaled, dtype=jnp.float32)


def rotate(vectors, angles):
    half_dim = vectors.shape[-1] // 2
    cosine = jnp.cos(angles)
    sine = jnp.sin(angles)
    first = vectors[..., :half_dim]
    second = vectors[..., half_dim:]
    return jnp.concatenate(
        [first * cosine - second * sine, second * cosine + first * sine], axis=-1
    )


def finish(query_sum, key_sum, value_sum, square_sum, positions):
    inv_rms = lax.rsqrt(square_sum / MODEL_WIDTH + EPSILON)[:, None]
    angles = positions.astype(jnp.float32)[:, None, None] * rotary_rates(HEAD_SIZE)[None, None, :]
    counted = query_sum.shape[0]
    query_rows = (
        rotate((query_sum * inv_rms).reshape(counted, -1, HEAD_SIZE), angles)
        .astype(jnp.bfloat16)
        .reshape(counted, -1)
    )
    recent_keys = (
        rotate((key_sum * inv_rms).reshape(counted, -1, HEAD_SIZE), angles)
        .astype(jnp.bfloat16)
        .reshape(counted, -1)
    )
    recent_values = (value_sum * inv_rms).astype(jnp.bfloat16)
    return (query_rows, recent_keys, recent_values)


def combine_parts(earlier, later):
    highest = jnp.maximum(earlier[0], later[0])
    first_scale = jnp.exp(earlier[0] - highest)
    second_scale = jnp.exp(later[0] - highest)
    return (
        highest,
        first_scale * earlier[1] + second_scale * later[1],
        first_scale[..., None] * earlier[2] + second_scale[..., None] * later[2],
    )


def local(
    token_ids,
    lengths,
    norm_gain,
    emb_table,
    q_weight,
    key_matrix,
    value_matrix,
    o_weight,
    key_cache,
    value_cache,
):
    tp_count = lax.axis_size("tp")
    seq_rank = lax.axis_index("seq")
    tp_rank = lax.axis_index("tp")
    count_of_rows = NEW_TOKENS * GAME_COUNT * CANDIDATE_MOVES
    group_size = QUERY_HEADS // KEY_HEADS
    scale = HEAD_SIZE ** (-0.5)
    local_heads = key_matrix.shape[1] // HEAD_SIZE
    shard_len = key_cache.shape[1]
    flat_ids = token_ids.reshape(count_of_rows)
    vocab_local = emb_table.shape[0]
    offset = flat_ids - (seq_rank * tp_count + tp_rank) * vocab_local
    inside = (offset >= 0) & (offset < vocab_local)
    picked = jnp.take(emb_table, jnp.clip(offset, 0, vocab_local - 1), axis=0)
    picked = jnp.where(inside[:, None], picked, jnp.zeros((), jnp.bfloat16))
    columns = lax.psum_scatter(picked, "seq", scatter_dimension=1, tiled=True).astype(jnp.float32)
    embedded = lax.psum(columns.astype(jnp.bfloat16), "tp").astype(jnp.float32)
    local_squares = jnp.sum(embedded * embedded, axis=-1)
    normed = (embedded * norm_gain.astype(jnp.float32)).astype(jnp.bfloat16)
    query_part = jnp.dot(normed, q_weight, preferred_element_type=jnp.float32)
    key_part = jnp.dot(normed, key_matrix, preferred_element_type=jnp.float32)
    value_part = jnp.dot(normed, value_matrix, preferred_element_type=jnp.float32)
    positions = (
        lengths[None, :, None]
        + jnp.arange(NEW_TOKENS, dtype=jnp.int32)[:, None, None]
        + jnp.zeros((NEW_TOKENS, GAME_COUNT, CANDIDATE_MOVES), jnp.int32)
    ).reshape(count_of_rows)
    query_sum, key_sum, value_sum, square_sum = lax.psum(
        (query_part, key_part, value_part, local_squares), "seq"
    )
    query_rows, recent_keys, recent_values = finish(
        query_sum, key_sum, value_sum, square_sum, positions
    )
    query_groups = query_rows.reshape(
        NEW_TOKENS, GAME_COUNT, CANDIDATE_MOVES, local_heads, group_size, HEAD_SIZE
    )
    grouped = query_groups.transpose(1, 3, 0, 2, 4, 5).reshape(
        GAME_COUNT, local_heads, -1, HEAD_SIZE
    )
    scores = (
        jnp.einsum("ghqd,gkhd->ghqk", grouped, key_cache, preferred_element_type=jnp.float32)
        * scale
    )
    cache_pos = seq_rank * shard_len + jnp.arange(shard_len, dtype=jnp.int32)
    live = (cache_pos[None, :] < lengths[:, None])[:, None, None, :]
    masked = jnp.where(live, scores, FLOOR)
    cache_peak = jnp.max(masked, axis=-1)
    shifted = jnp.where(live, jnp.exp(masked - cache_peak[..., None]), 0.0)
    cache_denominator = jnp.sum(shifted, axis=-1)
    cache_result = jnp.einsum(
        "ghqk,gkhd->ghqd",
        shifted.astype(jnp.bfloat16),
        value_cache,
        preferred_element_type=jnp.float32,
    )
    fresh_keys = recent_keys.reshape(
        NEW_TOKENS, GAME_COUNT, CANDIDATE_MOVES, local_heads, HEAD_SIZE
    )
    fresh_values = recent_values.reshape(
        NEW_TOKENS, GAME_COUNT, CANDIDATE_MOVES, local_heads, HEAD_SIZE
    )
    fresh_scores = (
        jnp.einsum(
            "agchjd,bgchd->agchjb", query_groups, fresh_keys, preferred_element_type=jnp.float32
        )
        * scale
    )
    causal = (
        jnp.arange(NEW_TOKENS, dtype=jnp.int32)[:, None]
        >= jnp.arange(NEW_TOKENS, dtype=jnp.int32)[None, :]
    )[:, None, None, None, None, :]
    fresh_masked = jnp.where(causal, fresh_scores, FLOOR)
    fresh_max = jnp.max(fresh_masked, axis=-1)
    fresh_shifted = jnp.where(causal, jnp.exp(fresh_masked - fresh_max[..., None]), 0.0)
    fresh_total = jnp.sum(fresh_shifted, axis=-1)
    fresh_out = jnp.einsum(
        "agchjb,bgchd->agchjd",
        fresh_shifted.astype(jnp.bfloat16),
        fresh_values,
        preferred_element_type=jnp.float32,
    )
    fresh_max = fresh_max.transpose(1, 3, 0, 2, 4).reshape(GAME_COUNT, local_heads, -1)
    fresh_total = fresh_total.transpose(1, 3, 0, 2, 4).reshape(GAME_COUNT, local_heads, -1)
    fresh_out = fresh_out.transpose(1, 3, 0, 2, 4, 5).reshape(
        GAME_COUNT, local_heads, -1, HEAD_SIZE
    )
    leading = seq_rank == 0
    joined = combine_parts(
        (cache_peak, cache_denominator, cache_result),
        (
            jnp.where(leading, fresh_max, FLOOR),
            jnp.where(leading, fresh_total, 0.0),
            jnp.where(leading, fresh_out, 0.0),
        ),
    )
    flat_rows = GAME_COUNT * local_heads * NEW_TOKENS * CANDIDATE_MOVES * group_size
    maxima = joined[0].reshape(1, flat_rows)
    totals = joined[1].reshape(1, flat_rows)
    summed = joined[2].reshape(1, flat_rows, HEAD_SIZE)
    merged_output = merged((maxima, totals, summed), "seq", combine_parts)
    context_vectors = (
        (merged_output[2] / merged_output[1][..., None])
        .astype(jnp.bfloat16)
        .reshape(flat_rows, HEAD_SIZE)
    )
    context_rows = (
        context_vectors.reshape(
            GAME_COUNT, local_heads, NEW_TOKENS, CANDIDATE_MOVES, group_size, HEAD_SIZE
        )
        .transpose(2, 0, 3, 1, 4, 5)
        .reshape(count_of_rows, -1)
    )
    return lax.psum_scatter(
        jnp.dot(context_rows, o_weight, preferred_element_type=jnp.float32).astype(jnp.bfloat16),
        "tp",
        scatter_dimension=0,
        tiled=True,
    )


def solution(mesh):
    placed = (
        P(),
        P(),
        P("seq"),
        P(("seq", "tp"), None),
        P("seq", "tp"),
        P("seq", "tp"),
        P("seq", "tp"),
        P("tp", "seq"),
        P(None, "seq", "tp", None),
        P(None, "seq", "tp", None),
    )
    return jax.shard_map(
        local, mesh=mesh, in_specs=placed, out_specs=P("tp", "seq"), check_vma=False
    )
```

profile of v0, /device:TPU:1, one launch (start us, length us, event | category | flops | bytes accessed | tf_op | source)
XLA Modules:
  0.0 486.4 jit_solution(4092522844973889592)
XLA Ops:
  6.6 0.8 compare_and_fusion
  7.5 0.7 subtract_clamp_fusion
  8.4 4.1 gather_fusion
  12.5 0.9 select_select_fusion
  13.7 0.1 multiply_cosine_fusion.1
  14.0 86.4 %reduce-scatter.2.cloned.1.call-done = bf16[32,256]{1,0:T(8,128)(2,1)} async-done(((bf16[32,8192]{1,0:T(8,128)(2,1)}), bf16[32,256]{1,0:T(8,128)(2,1)}) %reduce-scatter.2.cloned.1.call-update) | async-done | bytes 16400 | tf_op jit(solution)/shard_map/reduce_scatter | solution.py:114
  100.4 23.3 %psum.35 = bf16[32,256]{1,0:T(8,128)(2,1)S(1)} all-reduce(bf16[32,256]{1,0:T(8,128)(2,1)} %reduce-scatter.2.cloned.1.call-done), channel_id=1, replica_groups=mesh['seq'=32,'tp'=8] {'tp'}, use_global_device_ids=true, to_apply=%region_1.2 | all-reduce | flops 8192 | bytes 32768 | tf_op jit(solution)/shard_map/psum | solution.py:115
  123.7 0.1 fusion.30
  123.8 0.1 fusion.43
  123.9 0.1 fusion.41
  124.1 127.6 %all-reduce.1 = (f32[32]{0:T(128)S(1)}, f32[32,128]{1,0:T(8,128)S(1)}, f32[32,128]{1,0:T(8,128)S(1)}) all-reduce(f32[32]{0:T(128)S(1)} %fusion.30, f32[32,128]{1,0:T(8,128)S(1)} %fusion.43, f32[32,128]{1,0:T(8,128)S(1)} %fusion.41), channel_id=1, replica_groups=mesh['seq'=32,'tp'=8] {'seq'}, use_global_device_ids=true, to_apply=%region_4.5 | all-reduce | flops 8224 | bytes 65792 | tf_op jit(solution)/shard_map/psum | solution.py:126
  251.6 0.8 fusion.45
  252.6 0.1 fusion.36
  252.8 108.9 %all-reduce.4.cloned.1.call-done = f32[32,1024]{1,0:T(8,128)} async-done(((f32[32,1024]{1,0:T(8,128)}), f32[32,1024]{1,0:T(8,128)}) %all-reduce.4.cloned.1.call-update) | async-done | bytes 131088 | tf_op jit(solution)/shard_map/psum | solution.py:126
  361.7 1.0 multiply_bitcast_fusion
  362.8 0.1 subtract_convert_fusion
  362.9 0.5 fusion.58
  363.4 0.1 fusion.50
  363.8 0.3 fusion.13
  364.1 0.8 fusion.59
  365.0 1.9 copy-done.1
  366.9 1.6 fusion.19
  368.5 0.6 dynamic-slice
  370.0 3.1 fusion.5
  373.1 25.1 %all_gather.10 = f32[32,1,256]{2,1,0:T(1,128)S(1)} all-gather(f32[1,1,256]{2,1,0:T(1,128)S(1)} %get-tuple-element.205), channel_id=1, replica_groups=mesh['seq'=32,'tp'=8] {'seq'}, dimensions={0}, use_global_device_ids=true | all-gather | bytes 33792 | tf_op jit(solution)/shard_map/all_gather | solution.py:21
  398.2 21.4 %all_gather.9 = f32[32,1,256]{2,1,0:T(1,128)S(1)} all-gather(f32[1,1,256]{2,1,0:T(1,128)S(1)} %get-tuple-element.206), channel_id=1, replica_groups=mesh['seq'=32,'tp'=8] {'seq'}, dimensions={0}, use_global_device_ids=true | all-gather | bytes 33792 | tf_op jit(solution)/shard_map/all_gather | solution.py:21
  419.6 0.4 all-gather.2.cloned.1.call-done
  420.0 0.9 slice_bitcast_fusion
  420.9 34.8 %while.19 = (s32[]{:T(128)}, f32[1,256]{1,0:T(1,128)S(1)}, f32[1,256]{1,0:T(1,128)S(1)}, f32[1,256,128]{2,1,0:T(8,128)S(1)}, f32[32,1,256]{2,1,0:T(1,128)S(1)}, ...) while((s32[]{:T(128)}, f32[1,256]{1,0:T(1,128)S(1)}, ...), condition=%wide.region_12.13_spmd, body=%wide.region_11.12_spmd.sunk | while | flops 99845 | bytes 403599 | solution.py:26
  421.0 1.1 fusion.68
  422.1 1.1 fusion.68
  423.2 1.1 fusion.68
  424.4 1.1 fusion.68
  425.5 1.1 fusion.68
  426.6 1.1 fusion.68
  427.7 1.1 fusion.68
  428.9 1.1 fusion.68
  430.0 1.1 fusion.68
  431.1 1.1 fusion.68
  432.2 1.1 fusion.68
  433.3 1.1 fusion.68
  434.5 1.1 fusion.68
  435.6 1.1 fusion.68
  436.7 1.1 fusion.68
  437.8 1.1 fusion.68
  439.0 1.1 fusion.68
  440.1 1.1 fusion.68
  441.2 1.1 fusion.68
  442.3 1.1 fusion.68
  443.5 1.1 fusion.68
  444.6 1.1 fusion.68
  445.7 1.1 fusion.68
  446.8 1.1 fusion.68
  448.0 1.1 fusion.68
  449.1 1.1 fusion.68
  450.2 1.1 fusion.68
  451.3 1.1 fusion.68
  452.5 1.1 fusion.68
  453.6 1.1 fusion.68
  454.7 1.1 fusion.68
  455.8 0.1 divide_convert_fusion
  455.9 0.2 convolution_convert_fusion
  456.1 23.1 %all-reduce = bf16[32,256]{1,0:T(8,128)(2,1)S(1)} all-reduce(bf16[32,256]{1,0:T(8,128)(2,1)S(1)} %convolution_convert_fusion), channel_id=3, replica_groups=mesh['seq'=32,'tp'=8] {'tp'}, use_global_device_ids=true, to_apply=%region_13.14.clone | all-reduce | flops 8192 | bytes 32768
  479.3 0.6 constant_dynamic-slice_fusion.1
  (90 shorter events, 2.2 us)
Async XLA Ops:
  6.5 357.5 %copy-start = (bf16[2,4096,1,128]{3,1,2,0:T(8,128)(2,1)S(1)}, bf16[2,4096,1,128]{3,1,2,0:T(8,128)(2,1)}, u32[]{:S(2)}) copy-start(bf16[2,4096,1,128]{3,1,2,0:T(8,128)(2,1)} %param.21) | copy-start | bytes 6291460
  6.5 7.2 %copy-start.6 = (f32[64]{0:T(128)S(1)}, f32[64]{0:T(128)}, u32[]{:S(2)}) copy-start(f32[64]{0:T(128)} %constant.103.clone) | copy-start | bytes 772
  6.5 7.0 %copy-start.9 = (bf16[256]{0:T(256)(128)(2,1)S(1)}, bf16[256]{0:T(256)(128)(2,1)}, u32[]{:S(2)}) copy-start(bf16[256]{0:T(256)(128)(2,1)} %param.15) | copy-start | bytes 1540
  6.5 7.0 %copy-start.7 = (s32[2]{0:T(128)S(1)}, s32[2]{0:T(128)}, u32[]{:S(2)}) copy-start(s32[2]{0:T(128)} %param.14) | copy-start | bytes 28
  6.5 117.3 %copy-start.4 = (bf16[256,128]{1,0:T(8,128)(2,1)S(1)}, bf16[256,128]{1,0:T(8,128)(2,1)}, u32[]{:S(2)}) copy-start(bf16[256,128]{1,0:T(8,128)(2,1)} %param.18) | copy-start | bytes 196612
  6.5 117.4 %copy-start.5 = (bf16[256,128]{1,0:T(8,128)(2,1)S(1)}, bf16[256,128]{1,0:T(8,128)(2,1)}, u32[]{:S(2)}) copy-start(bf16[256,128]{1,0:T(8,128)(2,1)} %param.19) | copy-start | bytes 196612
  6.6 245.1 %copy-start.3 = (bf16[256,1024]{1,0:T(8,128)(2,1)S(1)}, bf16[256,1024]{1,0:T(8,128)(2,1)}, u32[]{:S(2)}) copy-start(bf16[256,1024]{1,0:T(8,128)(2,1)} %param.17) | copy-start | bytes 1572868
  6.6 93.8 %reduce-scatter.2.cloned.1.call-start = ((), (), s32[]{:S(2)}) async-start(), calls=%async_computation.1 | async-start | bytes 540672 | tf_op jit(solution)/shard_map/reduce_scatter | solution.py:114
  13.5 348.3 %all-reduce.4.cloned.1.call-start = ((), (), s32[]{:S(2)}) async-start(), calls=%async_computation.2 | async-start | bytes 262144 | tf_op jit(solution)/shard_map/psum | solution.py:126
  252.5 167.5 %all-gather.2.cloned.1.call-start = ((), (), s32[]{:S(2)}) async-start(), calls=%async_computation.3 | async-start | bytes 4325376 | tf_op jit(solution)/shard_map/all_gather | solution.py:21
  363.6 3.3 copy-start.8
  364.9 2.0 copy-start.1
  364.9 3.6 copy-start.10
  368.5 87.5 %copy-start.2 = (bf16[1024,256]{1,0:T(8,128)(2,1)S(1)}, bf16[1024,256]{1,0:T(8,128)(2,1)}, u32[]{:S(2)}) copy-start(bf16[1024,256]{1,0:T(8,128)(2,1)} %param.20) | copy-start | bytes 1572868
Sparse Core Ops, SparseCore 0:
  13.6 86.7 reduce-scatter.1
  252.6 109.0 all-reduce.3
  368.6 51.3 all-gather.1
where the time goes:
time: 493 us; the launch traced here: 486 us
  blocking collectives  220 us (45%)
  waiting for transfers between devices  196 us (40%)
  other arithmetic  41.7 us (8%)
  between operations  14 us (3%)
  local copies, waits for them, and re-layouts  8.94 us (2%)
    psum x1, blocking collectives, local(): lax.psum((query_part, key_part, value_part, local_squares), 'seq')  128 us
    psum x1, waiting for transfers between devices, local(): lax.psum((query_part, key_part, value_part, local_squares), 'seq')  109 us
    reduce_scatter x1, waiting for transfers between devices, local(): lax.psum_scatter(picked, 'seq', scatter_dimension=1, tiled=True)  86.4 us
    all_gather x2, blocking collectives, merged(): gathered = jax.tree.map(lambda a: lax.all_gather(a, axis), part)  46.5 us
    add x31, other arithmetic, combine_parts(): first_scale[..., None] * earlier[2] + second_scale[..., None] * later[2]  33.2 us
    psum x1, blocking collectives, local(): embedded = lax.psum(columns.astype(jnp.bfloat16), 'tp').astype(jnp.float32)  23.3 us
    unnamed x1, blocking collectives  23.1 us
  transfers between devices with their start and end apart: 3, of which 3 were waited for; matrix products, arithmetic and copies ran while one was open for 1% of the time, Pallas kernels for 0%

commit v1 on v0

v1 whole, which is shorter than its diff:
```python
import functools

import jax
import jax.numpy as jnp
import numpy as np
from jax import lax
from jax.experimental import pallas as pl
from jax.experimental.pallas import tpu as pltpu
from jax.sharding import PartitionSpec as P

MODEL_WIDTH = 8192
QUERY_HEADS = 64
KEY_HEADS = 8
HEAD_SIZE = 128
GAME_COUNT = 2
CANDIDATE_MOVES = 8
NEW_TOKENS = 2
ROWS = NEW_TOKENS * GAME_COUNT * CANDIDATE_MOVES
GROUP = QUERY_HEADS // KEY_HEADS

EPSILON = 1e-05
FLOOR = -1e30
LOWEST = -1e29
LOG2E = 1.4426950408889634
MESH = pl.DeviceIdType.MESH
F32 = jnp.float32
BF16 = jnp.bfloat16


def rotary_rates(head_dim):
    half_dim = head_dim // 2
    plain_rate = 500000.0 ** (-(np.arange(half_dim) * 2.0) / head_dim)
    wave_len = 2.0 * np.pi / plain_rate
    blend = (8192.0 / wave_len - 1.0) / 3.0
    scaled = np.where(
        wave_len < 2048.0,
        plain_rate,
        np.where(
            wave_len > 8192.0,
            plain_rate / 8.0,
            (1.0 - blend) * plain_rate / 8.0 + blend * plain_rate,
        ),
    )
    return np.concatenate([scaled, scaled]).astype(np.float32).reshape(1, head_dim)


def rounded(x):
    return x.astype(BF16).astype(F32)


def in_three(x):
    high = rounded(x)
    middle = rounded(x - high)
    return high, middle, rounded(x - high - middle)


def kernel(
    ids,
    lengths,
    gain,
    rates,
    emb,
    q_weight,
    key_matrix,
    value_matrix,
    o_weight,
    key_cache,
    value_cache,
    out,
    table,
    qw,
    kw,
    vw,
    ow,
    kc,
    vc,
    send1,
    recv1,
    send2,
    recv2,
    spread,
    send3,
    recv3,
    rows,
    send5,
    recv5,
    send6,
    recv6,
    send7,
    recv7,
    table_sems,
    load_sems,
    send_sems,
    recv_sems,
):
    seq, tp = lax.axis_size("seq"), lax.axis_size("tp")
    s, t = lax.axis_index("seq"), lax.axis_index("tp")
    width = gain.shape[0]
    vocab_local = emb.shape[0]
    shard_len = key_cache.shape[1]
    scale = HEAD_SIZE ** (-0.5)

    y, x, core = lax.div(s, 8), lax.rem(lax.div(s, 2), 4), lax.rem(s, 2)

    def moved(dy, dx, dc):
        return (lax.rem(y + dy, 4) * 4 + lax.rem(x + dx, 4)) * 2 + lax.rem(core + dc, 2)

    steps = [(dy, dx, dc) for dy in range(4) for dx in range(4) for dc in range(2)]
    steps.sort(key=lambda d: -10 * (min(d[0], 4 - d[0]) + min(d[1], 4 - d[1])) - d[2])
    seq_peers = [moved(*d) for d in steps[:-1]]
    tp_peers = [lax.rem(t + d, tp) for d in (4, 3, 5, 2, 6, 1, 7)]

    barrier = pltpu.get_barrier_semaphore()

    for device in [(peer, t) for peer in seq_peers] + [(s, peer) for peer in tp_peers]:
        pl.semaphore_signal(barrier, inc=1, device_id=device, device_id_type=MESH)

    def table_copy(chunk):
        return pltpu.make_async_copy(
            emb.at[:, pl.ds(pl.multiple_of(chunk * width, width), width)],
            table.at[chunk],
            table_sems.at[chunk],
        )

    for peer in seq_peers + [s]:
        table_copy(peer).start()
    loads = [
        pltpu.make_async_copy(src, dst, load_sems.at[i])
        for i, (src, dst) in enumerate(
            [
                (q_weight, qw),
                (key_matrix, kw),
                (value_matrix, vw),
                (key_cache, kc),
                (value_cache, vc),
                (o_weight, ow),
            ]
        )
    ]
    pending, loaded = [], set()

    def need(*names):
        for i in names:
            loads[i].wait()
            loaded.add(i)

    first_id = (s * tp + t) * vocab_local
    row_of = lax.broadcasted_iota(jnp.int32, (ROWS, vocab_local), 0)
    wanted = jnp.full((ROWS, vocab_local), -1, jnp.int32)
    for r in range(ROWS):
        token = ids[r // 16, (r // 8) % 2, r % 8]
        wanted = jnp.where(row_of == r, token - first_id, wanted)
    one_hot = jnp.where(
        wanted == lax.broadcasted_iota(jnp.int32, (ROWS, vocab_local), 1), 1.0, 0.0
    ).astype(BF16)

    def picked(chunk):
        table_copy(chunk).wait()
        return jnp.dot(one_hot, table[chunk], preferred_element_type=F32).astype(BF16)

    def scatter_copy(phase, source, target, device):
        return pltpu.make_async_remote_copy(
            src_ref=source,
            dst_ref=target,
            send_sem=send_sems.at[phase],
            recv_sem=recv_sems.at[phase],
            device_id=device,
            device_id_type=MESH,
        )

    def await_all(phase, buffer, count):
        part = buffer.at[pl.ds(0, count)]
        pltpu.make_async_copy(part, part, recv_sems.at[phase]).wait()

    def await_sent(phase, buffer, count):
        part = buffer.at[pl.ds(0, count)]
        pltpu.make_async_copy(part, part, send_sems.at[phase]).wait()

    pl.semaphore_wait(barrier, seq + tp - 2)

    for peer in seq_peers:
        send1[peer] = picked(peer)
        scatter_copy(0, send1.at[peer], recv1.at[s], (peer, t)).start()
    pending.append(lambda: await_sent(0, send1, seq - 1))
    recv1[s] = picked(s)
    for load in loads:
        load.start()
    await_all(0, recv1, seq - 1)

    found = jnp.sum(recv1[...].astype(F32), axis=0).astype(BF16)
    send2[...] = found

    for peer in tp_peers:
        scatter_copy(1, send2, recv2.at[t], (s, peer)).start()
    pending.append(lambda: await_sent(1, recv2, tp - 1))
    recv2[t] = found
    await_all(1, recv2, tp - 1)
    embedded = jnp.sum(recv2[...].astype(F32), axis=0)

    squares = jnp.sum(embedded * embedded, axis=-1, keepdims=True)
    normed = (embedded * gain[...].astype(F32)[None, :]).astype(BF16)
    need(0, 1, 2)
    query_part = jnp.dot(normed, qw[...], preferred_element_type=F32)
    key_part = jnp.dot(normed, kw[...], preferred_element_type=F32)
    value_part = jnp.dot(normed, vw[...], preferred_element_type=F32)
    for j in range(GROUP):
        spread[pl.ds(j, ROWS, stride=16), :] = query_part[:, j * HEAD_SIZE : (j + 1) * HEAD_SIZE]
    spread[pl.ds(8, ROWS, stride=16), :] = key_part
    spread[pl.ds(9, ROWS, stride=16), :] = value_part
    for j in range(10, 16):
        spread[pl.ds(j, ROWS, stride=16), :] = jnp.broadcast_to(squares, (ROWS, HEAD_SIZE))
    send3[...] = spread[...].reshape(ROWS, 16, HEAD_SIZE).astype(BF16)

    for peer in seq_peers:
        scatter_copy(2, send3.at[peer], recv3.at[s], (peer, t)).start()
    pending.append(lambda: await_sent(2, send3, seq - 1))
    recv3[s] = send3[s]
    game = lax.rem(lax.div(s, CANDIDATE_MOVES), GAME_COUNT)
    step = lax.div(s, GAME_COUNT * CANDIDATE_MOVES)
    position = (lengths[game] + step).astype(F32)
    angles = position * rates[...]
    lane = lax.broadcasted_iota(jnp.int32, (1, HEAD_SIZE), 1)
    cosine = jnp.cos(angles)
    sine = jnp.sin(angles)
    sine = jnp.where(lane < HEAD_SIZE // 2, -sine, sine)
    await_all(2, recv3, seq - 1)

    sums = jnp.sum(recv3[...].astype(F32), axis=0)
    inv_rms = lax.rsqrt(sums[10:11, :] / MODEL_WIDTH + EPSILON)
    scaled = sums * inv_rms
    turned = scaled * cosine + pltpu.roll(scaled, HEAD_SIZE // 2, 1) * sine
    place = lax.broadcasted_iota(jnp.int32, (16, HEAD_SIZE), 0)
    own = jnp.where(place < 9, turned, scaled).astype(BF16)
    rows[s] = own

    for peer in seq_peers:
        scatter_copy(3, rows.at[s], rows.at[s], (peer, t)).start()
    pending.append(lambda: await_sent(3, rows, seq - 1))
    own_queries = own.astype(F32)[:8, :]
    need(3, 4)
    await_all(3, rows, seq - 1)

    factor = scale * LOG2E
    for g in range(GAME_COUNT):
        halves = [
            rows[pl.ds(16 * a + 8 * g, 8)].astype(F32)[:, :8, :].reshape(64, HEAD_SIZE)
            for a in range(NEW_TOKENS)
        ]
        queries = jnp.concatenate(halves, axis=0).astype(BF16)
        scores = lax.dot_general(
            queries, kc[g], (((1,), (1,)), ((), ())), preferred_element_type=F32
        )
        slot = s * shard_len + lax.broadcasted_iota(jnp.int32, (1, shard_len), 1)
        masked = jnp.where(slot < lengths[g], scores * factor, FLOOR)
        top = jnp.maximum(jnp.max(masked, axis=-1, keepdims=True), LOWEST)
        shifted = jnp.exp2(masked - top)
        total = jnp.sum(shifted, axis=-1, keepdims=True)
        summed = jnp.dot(shifted.astype(BF16), vc[g], preferred_element_type=F32)
        lanes = lax.broadcasted_iota(jnp.int32, (128, HEAD_SIZE), 1)
        packed = jnp.zeros((128, HEAD_SIZE), F32)
        for i, piece in enumerate(in_three(top) + in_three(total)):
            packed = jnp.where(lanes == i, piece, packed)
        message = jnp.concatenate(
            [summed.reshape(16, 8, HEAD_SIZE), packed.reshape(16, 8, HEAD_SIZE)], axis=1
        ).astype(BF16)
        for a in range(NEW_TOKENS):
            send5[pl.ds(16 * a + 8 * g, 8)] = message[8 * a : 8 * a + 8]

    for peer in seq_peers:
        scatter_copy(4, send5.at[peer], recv5.at[s], (peer, t)).start()
    pending.append(lambda: await_sent(4, send5, seq - 1))
    recv5[s] = send5[s]

    twin = lax.rem(s, GAME_COUNT * CANDIDATE_MOVES)
    firsts = rows[pl.ds(twin, 1)].astype(F32)[0]
    seconds = rows[pl.ds(twin + 16, 1)].astype(F32)[0]
    score_a = jnp.sum(own_queries * firsts[8:9, :], axis=-1, keepdims=True) * factor
    score_b = jnp.sum(own_queries * seconds[8:9, :], axis=-1, keepdims=True) * factor
    score_b = jnp.where(step >= 1, score_b, FLOOR)
    fresh_top = jnp.maximum(score_a, score_b)
    fresh_a = jnp.exp2(score_a - fresh_top)
    fresh_b = jnp.exp2(score_b - fresh_top)
    fresh_total = fresh_a + fresh_b
    fresh_sum = rounded(fresh_a) * firsts[9:10, :] + rounded(fresh_b) * seconds[9:10, :]
    pick = lax.broadcasted_iota(jnp.int32, (HEAD_SIZE, 2 * HEAD_SIZE), 0)
    side = lax.broadcasted_iota(jnp.int32, (HEAD_SIZE, 2 * HEAD_SIZE), 1) >= HEAD_SIZE
    pick = pick - jnp.where(side, 3, 0)
    picker = jnp.where((pick >= 0) & (pick < 3), 1.0, 0.0).astype(BF16)
    await_all(4, recv5, seq - 1)

    parts = recv5[...].astype(F32)
    unpacked = jnp.dot(
        parts[:, 8:, :].reshape(seq * 8, HEAD_SIZE).astype(BF16),
        picker,
        preferred_element_type=F32,
    )
    tops = unpacked[:, :HEAD_SIZE].reshape(seq, 8, HEAD_SIZE)
    totals = unpacked[:, HEAD_SIZE:].reshape(seq, 8, HEAD_SIZE)
    highest = jnp.maximum(jnp.max(tops, axis=0), fresh_top)
    shares = jnp.exp2(tops - highest[None])
    fresh_share = jnp.exp2(fresh_top - highest)
    whole = jnp.sum(shares * totals, axis=0) + fresh_share * fresh_total
    summed = jnp.sum(shares * parts[:, :8, :], axis=0) + fresh_share * fresh_sum
    context = rounded(summed / whole)
    send6[...] = context
    here = pl.ds(pl.multiple_of(s * 8, 8), 8)
    recv6[here, :] = context

    for peer in seq_peers:
        scatter_copy(5, send6, recv6.at[here], (peer, t)).start()
    pending.append(lambda: await_sent(5, recv6, (seq - 1) * 8))
    need(5)
    await_all(5, recv6, (seq - 1) * 8)

    contexts = jnp.concatenate(
        [recv6[pl.ds(j, ROWS, stride=8), :] for j in range(GROUP)], axis=1
    ).astype(BF16)
    product = jnp.dot(contexts, ow[...], preferred_element_type=F32)
    share = ROWS // 8
    for z in range(8):
        send7[z, 0:share, :] = product[z * share : (z + 1) * share, :HEAD_SIZE]
        send7[z, share : 2 * share, :] = product[z * share : (z + 1) * share, HEAD_SIZE:]

    for peer in tp_peers:
        scatter_copy(6, send7.at[peer], recv7.at[t], (s, peer)).start()
    pending.append(lambda: await_sent(6, send7, tp - 1))
    recv7[t] = send7[t]
    await_all(6, recv7, tp - 1)
    result = jnp.sum(recv7[...], axis=0)
    out[...] = jnp.concatenate([result[:share], result[share:]], axis=1).astype(BF16)

    for wait in pending:
        wait()


def local(
    token_ids,
    lengths,
    norm_gain,
    emb_table,
    q_weight,
    key_matrix,
    value_matrix,
    o_weight,
    key_cache,
    value_cache,
):
    seq, tp = lax.axis_size("seq"), lax.axis_size("tp")
    width = emb_table.shape[1] // seq
    shard_len = key_cache.shape[1]
    vmem, smem, hbm = pltpu.VMEM, pltpu.SMEM, pltpu.HBM
    cache = (GAME_COUNT, shard_len, HEAD_SIZE)
    return pl.pallas_call(
        kernel,
        out_shape=jax.ShapeDtypeStruct((ROWS // tp, width), BF16),
        in_specs=[pl.BlockSpec(memory_space=m) for m in [smem, smem, vmem, vmem] + [hbm] * 7],
        out_specs=pl.BlockSpec(memory_space=vmem),
        scratch_shapes=[
            vmem((seq, emb_table.shape[0], width), BF16),
            vmem(q_weight.shape, BF16),
            vmem(key_matrix.shape, BF16),
            vmem(value_matrix.shape, BF16),
            vmem(o_weight.shape, BF16),
            vmem(cache, BF16),
            vmem(cache, BF16),
            vmem((seq, ROWS, width), BF16),
            vmem((seq, ROWS, width), BF16),
            vmem((ROWS, width), BF16),
            vmem((tp, ROWS, width), BF16),
            vmem((ROWS * 16, HEAD_SIZE), F32),
            vmem((ROWS, 16, HEAD_SIZE), BF16),
            vmem((seq, 16, HEAD_SIZE), BF16),
            vmem((ROWS, 16, HEAD_SIZE), BF16),
            vmem((ROWS, 16, HEAD_SIZE), BF16),
            vmem((seq, 16, HEAD_SIZE), BF16),
            vmem((8, HEAD_SIZE), F32),
            vmem((ROWS * 8, HEAD_SIZE), F32),
            vmem((tp, 8, HEAD_SIZE), F32),
            vmem((tp, 8, HEAD_SIZE), F32),
            pltpu.SemaphoreType.DMA((seq,)),
            pltpu.SemaphoreType.DMA((6,)),
            pltpu.SemaphoreType.DMA((7,)),
            pltpu.SemaphoreType.DMA((7,)),
        ],
        compiler_params=pltpu.CompilerParams(
            collective_id=0, has_side_effects=True, vmem_limit_bytes=60 * 1024 * 1024
        ),
    )(
        token_ids,
        lengths,
        norm_gain,
        jnp.asarray(rotary_rates(HEAD_SIZE)),
        emb_table,
        q_weight,
        key_matrix,
        value_matrix,
        o_weight,
        key_cache.reshape(cache),
        value_cache.reshape(cache),
    )


def solution(mesh):
    placed = (
        P(),
        P(),
        P("seq"),
        P(("seq", "tp"), None),
        P("seq", "tp"),
        P("seq", "tp"),
        P("seq", "tp"),
        P("tp", "seq"),
        P(None, "seq", "tp", None),
        P(None, "seq", "tp", None),
    )
    return jax.shard_map(
        local, mesh=mesh, in_specs=placed, out_specs=P("tp", "seq"), check_vma=False
    )
```

time: 493 us -> 54.7 us (0.11); the launches traced: 486 us -> 54.6 us
  blocking collectives: 220 us -> 0 us
  waiting for transfers between devices: 196 us -> 0 us
  Pallas kernels: 0 us -> 53.3 us
  other arithmetic: 41.7 us -> 0 us
  between operations: 14 us -> 0.01 us
  local copies, waits for them, and re-layouts: 8.94 us -> 1.26 us
    psum x2 -> x0, blocking collectives: 151 us -> none  [the longest x1 128 us: local(): lax.psum((query_part, key_part, value_part, local_squares), 'seq')]
    psum x1 -> x0, waiting for transfers between devices: 109 us -> none  [local(): lax.psum((query_part, key_part, value_part, local_squares), 'seq')]
    reduce_scatter x1 -> x0, waiting for transfers between devices: 86.4 us -> none  [local(): lax.psum_scatter(picked, 'seq', scatter_dimension=1, tiled=True)]
    pallas_call x0 -> x1, Pallas kernels: none -> 53.3 us  [local(): pl.pallas_call(kernel, out_shape=jax.ShapeDtypeStruct((ROWS // tp, width)...]
    all_gather x2 -> x0, blocking collectives: 46.5 us -> none  [merged(): gathered = jax.tree.map(lambda a: lax.all_gather(a, axis), part)]
    add x64 -> x0, other arithmetic: 34.1 us -> none  [the longest x31 33.2 us: combine_parts(): first_scale[..., None] * earlier[2] + second_scale[..., None] * later[2]]
    unnamed x1 -> x0, blocking collectives: 23.1 us -> none
  transfers between devices with their start and end apart: 3 -> 0, of which waited for: 3 -> 0; matrix products, arithmetic and copies ran while one was open for 1% -> 0% of each run, Pallas kernels for 0% -> 0%
where the time goes in v1:
time: 54.7 us; the launch traced here: 54.6 us
  Pallas kernels  53.3 us (97%)
  local copies, waits for them, and re-layouts  1.26 us (2%)
    pallas_call x1, Pallas kernels, local(): pl.pallas_call(kernel, out_shape=jax.ShapeDtypeStruct((ROWS // tp, width)...  53.3 us
    unnamed x1, local copies, waits for them, and re-layouts  1.26 us

profile of v1, /device:TPU:1, one launch (start us, length us, event | category | flops | bytes accessed | tf_op | source)
XLA Modules:
  0.0 54.6 jit_solution(689747239799851521)
XLA Ops:
  0.0 53.3 %shard_map.109 = bf16[4,256]{1,0:T(4,128)(2,1)} custom-call(s32[2,2,8]{2,1,0:T(2,128)} %ids.1, s32[2]{0:T(128)} %lengths.1, bf16[256]{0:T(256)(128)(2,1)} %gain.1, f32[1,128]{1,0:T(1,128)} %constant.2.clone.rates, bf16[256,8192]{1,0:T(8,128)(2,1)} %emb.1, bf16[256,1024]{1,0:T(8,128)(2,1)} %q_weight.1, bf16[256,128]{1,0:T(8,128)(2,1)} %key_matrix.1, ...), custom_call_target="tpu_custom_call" | custom-call | tf_op jit(solution)/shard_map/pallas_call | solution.py:353
  53.3 1.3 %copy.13 = bf16[4,256]{1,0:T(4,128)(2,1)} copy(bf16[4,256]{1,0:T(4,128)(2,1)} %shard_map.109) | data formatting | bytes 4096

commit v2 on v1

--- a/solution.py
+++ b/solution.py
@@ -22,6 +22,8 @@
 FLOOR = -1e30
 LOWEST = -1e29
 LOG2E = 1.4426950408889634
+SLOTS = 8
+GROUP_SLOTS = 16
 MESH = pl.DeviceIdType.MESH
 F32 = jnp.float32
 BF16 = jnp.bfloat16
@@ -55,6 +57,7 @@
 
 
 def kernel(
+    compact,
     ids,
     lengths,
     gain,
@@ -67,6 +70,7 @@
     key_cache,
     value_cache,
     out,
+    overflow,
     table,
     qw,
     kw,
@@ -115,15 +119,18 @@
     for device in [(peer, t) for peer in seq_peers] + [(s, peer) for peer in tp_peers]:
         pl.semaphore_signal(barrier, inc=1, device_id=device, device_id_type=MESH)
 
-    def table_copy(chunk):
-        return pltpu.make_async_copy(
-            emb.at[:, pl.ds(pl.multiple_of(chunk * width, width), width)],
-            table.at[chunk],
-            table_sems.at[chunk],
-        )
-
-    for peer in seq_peers + [s]:
-        table_copy(peer).start()
+    planes = [lax.rem(y + dy, 4) for dy in (2, 1, 3, 0)]
+    stripe = table.shape[2]
+    table_loads = [
+        pltpu.make_async_copy(
+            emb.at[:, pl.ds(pl.multiple_of(plane * stripe, stripe), stripe)],
+            table.at[i],
+            table_sems.at[i],
+        )
+        for i, plane in enumerate(planes)
+    ]
+    for load in table_loads:
+        load.start()
     loads = [
         pltpu.make_async_copy(src, dst, load_sems.at[i])
         for i, (src, dst) in enumerate(
@@ -144,19 +151,72 @@
             loads[i].wait()
             loaded.add(i)
 
+    tokens = [ids[r // 16, (r // 8) % 2, r % 8] for r in range(ROWS)]
+    down = jnp.zeros((ROWS, HEAD_SIZE), jnp.int32)
+    along = jnp.zeros((ROWS, HEAD_SIZE), jnp.int32)
+    rows_at = lax.broadcasted_iota(jnp.int32, (ROWS, HEAD_SIZE), 0)
+    lanes_at = lax.broadcasted_iota(jnp.int32, (ROWS, HEAD_SIZE), 1)
+    for r, token in enumerate(tokens):
+        down = jnp.where(rows_at == r, token, down)
+        along = jnp.where(lanes_at == r, token, along)
+    in_block = vocab_local.bit_length() - 1
+    block_down, block_along = jnp.right_shift(down, in_block), jnp.right_shift(along, in_block)
+    plane_down, plane_along = block_down & (tp - 1), block_along & (tp - 1)
     first_id = (s * tp + t) * vocab_local
-    row_of = lax.broadcasted_iota(jnp.int32, (ROWS, vocab_local), 0)
-    wanted = jnp.full((ROWS, vocab_local), -1, jnp.int32)
-    for r in range(ROWS):
-        token = ids[r // 16, (r // 8) % 2, r % 8]
-        wanted = jnp.where(row_of == r, token - first_id, wanted)
-    one_hot = jnp.where(
-        wanted == lax.broadcasted_iota(jnp.int32, (ROWS, vocab_local), 1), 1.0, 0.0
+    token_rows = jnp.concatenate([down - first_id] * (vocab_local // HEAD_SIZE), axis=1)
+    hits = jnp.where(
+        token_rows == lax.broadcasted_iota(jnp.int32, (ROWS, vocab_local), 1), 1.0, 0.0
     ).astype(BF16)
-
-    def picked(chunk):
-        table_copy(chunk).wait()
-        return jnp.dot(one_hot, table[chunk], preferred_element_type=F32).astype(BF16)
+    if compact:
+        earlier, later = (lanes_at < rows_at), (rows_at < lanes_at)
+
+        def slots(there, here):
+            same = there == here
+            by_row = jnp.sum(jnp.where(same & earlier, 1.0, 0.0), axis=1, keepdims=True)
+            by_lane = jnp.sum(jnp.where(same & later, 1.0, 0.0), axis=0, keepdims=True)
+            return by_row.astype(jnp.int32), by_lane.astype(jnp.int32)
+
+        slot_down, slot_along = slots(block_down, block_along)
+        group_down, group_along = slots(plane_down, plane_along)
+        too_many = (jnp.max(slot_down) >= SLOTS) | (jnp.max(group_down) >= GROUP_SLOTS)
+        overflow[0] = jnp.where(too_many, 1, 0)
+        token_lane = lanes_at < ROWS
+        mine = (block_along == s * tp + t) & (slot_along == rows_at) & token_lane
+        mine = jnp.where(mine, 1.0, 0.0).astype(BF16)[:16, :ROWS]
+        one_hot = jnp.dot(mine, hits, preferred_element_type=F32).astype(BF16)
+        ours = (plane_along == t) & (group_along == rows_at) & token_lane
+        ours = jnp.where(ours, 1.0, 0.0).astype(BF16)[:GROUP_SLOTS, :ROWS]
+        spot = jnp.right_shift(block_down[:, :1], tp.bit_length() - 1) * 16 + slot_down
+        spots = lax.broadcasted_iota(jnp.int32, (ROWS, seq * 16), 1)
+        to_group = jnp.concatenate(
+            [
+                jnp.dot(
+                    ours,
+                    jnp.where(spots == spot + half * SLOTS, 1.0, 0.0).astype(BF16),
+                    preferred_element_type=F32,
+                )
+                for half in range(2)
+            ],
+            axis=0,
+        ).astype(BF16)
+        spot = plane_down[:, :1] * GROUP_SLOTS + group_down
+        to_rows = jnp.where(
+            lax.broadcasted_iota(jnp.int32, (ROWS, tp * GROUP_SLOTS), 1) == spot, 1.0, 0.0
+        ).astype(BF16)
+    else:
+        overflow[0] = 0
+        one_hot = hits
+
+    for i, plane in enumerate(planes):
+        table_loads[i].wait()
+        found = jnp.dot(one_hot, table[i], preferred_element_type=F32)
+        for j in range(stripe // width):
+            part = found[:, j * width : (j + 1) * width]
+            if compact:
+                part = jnp.concatenate(
+                    [part[:SLOTS, :HEAD_SIZE], part[:SLOTS, HEAD_SIZE:]], axis=0
+                )
+            send1[plane * (stripe // width) + j] = part.astype(BF16)
 
     def scatter_copy(phase, source, target, device):
         return pltpu.make_async_remote_copy(
@@ -179,23 +239,32 @@
     pl.semaphore_wait(barrier, seq + tp - 2)
 
     for peer in seq_peers:
-        send1[peer] = picked(peer)
         scatter_copy(0, send1.at[peer], recv1.at[s], (peer, t)).start()
     pending.append(lambda: await_sent(0, send1, seq - 1))
-    recv1[s] = picked(s)
+    recv1[s] = send1[s]
     for load in loads:
         load.start()
     await_all(0, recv1, seq - 1)
 
-    found = jnp.sum(recv1[...].astype(F32), axis=0).astype(BF16)
+    if compact:
+        found = jnp.dot(
+            to_group, recv1[...].reshape(seq * 16, HEAD_SIZE), preferred_element_type=F32
+        )
+        found = jnp.concatenate([found[:GROUP_SLOTS], found[GROUP_SLOTS:]], axis=1).astype(BF16)
+    else:
+        found = jnp.sum(recv1[...].astype(F32), axis=0).astype(BF16)
     send2[...] = found
-
     for peer in tp_peers:
         scatter_copy(1, send2, recv2.at[t], (s, peer)).start()
     pending.append(lambda: await_sent(1, recv2, tp - 1))
     recv2[t] = found
     await_all(1, recv2, tp - 1)
-    embedded = jnp.sum(recv2[...].astype(F32), axis=0)
+    if compact:
+        embedded = jnp.dot(
+            to_rows, recv2[...].reshape(tp * GROUP_SLOTS, width), preferred_element_type=F32
+        )
+    else:
+        embedded = jnp.sum(recv2[...].astype(F32), axis=0)
 
     squares = jnp.sum(embedded * embedded, axis=-1, keepdims=True)
     normed = (embedded * gain[...].astype(F32)[None, :]).astype(BF16)
@@ -347,45 +416,9 @@
 ):
     seq, tp = lax.axis_size("seq"), lax.axis_size("tp")
     width = emb_table.shape[1] // seq
-    shard_len = key_cache.shape[1]
+    cache = (GAME_COUNT, key_cache.shape[1], HEAD_SIZE)
     vmem, smem, hbm = pltpu.VMEM, pltpu.SMEM, pltpu.HBM
-    cache = (GAME_COUNT, shard_len, HEAD_SIZE)
-    return pl.pallas_call(
-        kernel,
-        out_shape=jax.ShapeDtypeStruct((ROWS // tp, width), BF16),
-        in_specs=[pl.BlockSpec(memory_space=m) for m in [smem, smem, vmem, vmem] + [hbm] * 7],
-        out_specs=pl.BlockSpec(memory_space=vmem),
-        scratch_shapes=[
-            vmem((seq, emb_table.shape[0], width), BF16),
-            vmem(q_weight.shape, BF16),
-            vmem(key_matrix.shape, BF16),
-            vmem(value_matrix.shape, BF16),
-            vmem(o_weight.shape, BF16),
-            vmem(cache, BF16),
-            vmem(cache, BF16),
-            vmem((seq, ROWS, width), BF16),
-            vmem((seq, ROWS, width), BF16),
-            vmem((ROWS, width), BF16),
-            vmem((tp, ROWS, width), BF16),
-            vmem((ROWS * 16, HEAD_SIZE), F32),
-            vmem((ROWS, 16, HEAD_SIZE), BF16),
-            vmem((seq, 16, HEAD_SIZE), BF16),
-            vmem((ROWS, 16, HEAD_SIZE), BF16),
-            vmem((ROWS, 16, HEAD_SIZE), BF16),
-            vmem((seq, 16, HEAD_SIZE), BF16),
-            vmem((8, HEAD_SIZE), F32),
-            vmem((ROWS * 8, HEAD_SIZE), F32),
-            vmem((tp, 8, HEAD_SIZE), F32),
-            vmem((tp, 8, HEAD_SIZE), F32),
-            pltpu.SemaphoreType.DMA((seq,)),
-            pltpu.SemaphoreType.DMA((6,)),
-            pltpu.SemaphoreType.DMA((7,)),
-            pltpu.SemaphoreType.DMA((7,)),
-        ],
-        compiler_params=pltpu.CompilerParams(
-            collective_id=0, has_side_effects=True, vmem_limit_bytes=60 * 1024 * 1024
-        ),
-    )(
+    operands = (
         token_ids,
         lengths,
         norm_gain,
@@ -398,6 +431,54 @@
         key_cache.reshape(cache),
         value_cache.reshape(cache),
     )
+
+    def run(compact):
+        row_message = (16, HEAD_SIZE) if compact else (ROWS, width)
+        group_message = (GROUP_SLOTS, width) if compact else (ROWS, width)
+        return pl.pallas_call(
+            functools.partial(kernel, compact),
+            out_shape=(
+                jax.ShapeDtypeStruct((ROWS // tp, width), BF16),
+                jax.ShapeDtypeStruct((1,), jnp.int32),
+            ),
+            in_specs=[pl.BlockSpec(memory_space=m) for m in [smem, smem, vmem, vmem] + [hbm] * 7],
+            out_specs=(pl.BlockSpec(memory_space=vmem), pl.BlockSpec(memory_space=smem)),
+            scratch_shapes=[
+                vmem((4, emb_table.shape[0], emb_table.shape[1] // 4), BF16),
+                vmem(q_weight.shape, BF16),
+                vmem(key_matrix.shape, BF16),
+                vmem(value_matrix.shape, BF16),
+                vmem(o_weight.shape, BF16),
+                vmem(cache, BF16),
+                vmem(cache, BF16),
+                vmem((seq,) + row_message, BF16),
+                vmem((seq,) + row_message, BF16),
+                vmem(group_message, BF16),
+                vmem((tp,) + group_message, BF16),
+                vmem((ROWS * 16, HEAD_SIZE), F32),
+                vmem((ROWS, 16, HEAD_SIZE), BF16),
+                vmem((seq, 16, HEAD_SIZE), BF16),
+                vmem((ROWS, 16, HEAD_SIZE), BF16),
+                vmem((ROWS, 16, HEAD_SIZE), BF16),
+                vmem((seq, 16, HEAD_SIZE), BF16),
+                vmem((8, HEAD_SIZE), F32),
+                vmem((ROWS * 8, HEAD_SIZE), F32),
+                vmem((tp, 8, HEAD_SIZE), F32),
+                vmem((tp, 8, HEAD_SIZE), F32),
+                pltpu.SemaphoreType.DMA((4,)),
+                pltpu.SemaphoreType.DMA((6,)),
+                pltpu.SemaphoreType.DMA((7,)),
+                pltpu.SemaphoreType.DMA((7,)),
+            ],
+            compiler_params=pltpu.CompilerParams(
+                collective_id=0 if compact else 1,
+                has_side_effects=True,
+                vmem_limit_bytes=64 * 1024 * 1024,
+            ),
+        )(*operands)
+
+    result, overflow = run(True)
+    return lax.cond(overflow[0] > 0, lambda: run(False)[0], lambda: result)
 
 
 def solution(mesh):

time: 54.7 us -> 50.3 us (0.920)
  Pallas kernels: 53.3 us -> 48.3 us
  between operations: 0.01 us -> 0.64 us
    pallas_call x1, Pallas kernels: 53.3 us -> 48.3 us  [run(): pl.pallas_call(functools.partial(kernel, compact), out_shape=(jax.ShapeDt...]
where the time goes in v2:
time: 50.3 us; the launch traced here: 50.2 us
  Pallas kernels  48.3 us (96%)
  local copies, waits for them, and re-layouts  1.24 us (2%)
  between operations  0.64 us (1%)
    pallas_call x1, Pallas kernels, run(): pl.pallas_call(functools.partial(kernel, compact), out_shape=(jax.ShapeDt...  48.3 us
    unnamed x1, local copies, waits for them, and re-layouts  1.24 us

profile of v2, /device:TPU:1, one launch (start us, length us, event | category | flops | bytes accessed | tf_op | source)
XLA Modules:
  0.0 50.2 jit_solution(16171161509382990008)
XLA Ops:
  0.0 48.3 %shard_map.111 = (bf16[4,256]{1,0:T(4,128)(2,1)}, s32[1]{0:T(128)}) custom-call(s32[2,2,8]{2,1,0:T(2,128)} %ids.1, s32[2]{0:T(128)} %lengths.1, bf16[256]{0:T(256)(128)(2,1)} %gain.1, f32[1,128]{1,0:T(1,128)} %constant.5.clone.rates, bf16[256,8192]{1,0:T(8,128)(2,1)} %emb.1, bf16[256,1024]{1,0:T(8,128)(2,1)} %q_weight.1, bf16[256,128]{1,0:T(8,128)(2,1)} %key_matrix.1, ...), custom_call_target="tpu_custom_call" | custom-call | tf_op jit(solution)/shard_map/pallas_call | solution.py:438
  48.9 1.2 %copy.17 = bf16[4,256]{1,0:T(4,128)(2,1)} copy(bf16[4,256]{1,0:T(4,128)(2,1)} %get-tuple-element.47) | data formatting | bytes 4096
  (1 shorter events, 0.0 us)

commit v3 on v2

--- a/solution.py
+++ b/solution.py
@@ -22,8 +22,9 @@
 FLOOR = -1e30
 LOWEST = -1e29
 LOG2E = 1.4426950408889634
-SLOTS = 8
-GROUP_SLOTS = 16
+SLOTS = 4
+GROUP_SLOTS = 12
+KEYS = 1024
 MESH = pl.DeviceIdType.MESH
 F32 = jnp.float32
 BF16 = jnp.bfloat16
@@ -72,9 +73,7 @@
     out,
     overflow,
     table,
-    qw,
-    kw,
-    vw,
+    weights,
     ow,
     kc,
     vc,
@@ -86,10 +85,12 @@
     send3,
     recv3,
     rows,
+    pair,
+    scores,
     send5,
     recv5,
-    send6,
     recv6,
+    wide,
     send7,
     recv7,
     table_sems,
@@ -101,6 +102,7 @@
     s, t = lax.axis_index("seq"), lax.axis_index("tp")
     width = gain.shape[0]
     vocab_local = emb.shape[0]
+    heads = q_weight.shape[1]
     shard_len = key_cache.shape[1]
     scale = HEAD_SIZE ** (-0.5)
 
@@ -113,11 +115,6 @@
     steps.sort(key=lambda d: -10 * (min(d[0], 4 - d[0]) + min(d[1], 4 - d[1])) - d[2])
     seq_peers = [moved(*d) for d in steps[:-1]]
     tp_peers = [lax.rem(t + d, tp) for d in (4, 3, 5, 2, 6, 1, 7)]
-
-    barrier = pltpu.get_barrier_semaphore()
-
-    for device in [(peer, t) for peer in seq_peers] + [(s, peer) for peer in tp_peers]:
-        pl.semaphore_signal(barrier, inc=1, device_id=device, device_id_type=MESH)
 
     planes = [lax.rem(y + dy, 4) for dy in (2, 1, 3, 0)]
     stripe = table.shape[2]
@@ -131,15 +128,23 @@
     ]
     for load in table_loads:
         load.start()
+
+    barrier = pltpu.get_barrier_semaphore()
+
+    greeted = [(s, peer) for peer in tp_peers]
+    greeted = greeted[:3] + [(peer, t) for peer in seq_peers[:22]] + greeted[3:]
+    for device in greeted + [(peer, t) for peer in seq_peers[22:]]:
+        pl.semaphore_signal(barrier, inc=1, device_id=device, device_id_type=MESH)
+
     loads = [
         pltpu.make_async_copy(src, dst, load_sems.at[i])
         for i, (src, dst) in enumerate(
             [
-                (q_weight, qw),
-                (key_matrix, kw),
-                (value_matrix, vw),
+                (q_weight, weights.at[:, pl.ds(0, heads)]),
+                (key_matrix, weights.at[:, pl.ds(heads, HEAD_SIZE)]),
+                (value_matrix, weights.at[:, pl.ds(heads + HEAD_SIZE, HEAD_SIZE)]),
                 (key_cache, kc),
-                (value_cache, vc),
+                (value_cache, vc.at[:, :, pl.ds(0, HEAD_SIZE)]),
                 (o_weight, ow),
             ]
         )
@@ -185,23 +190,24 @@
         mine = jnp.where(mine, 1.0, 0.0).astype(BF16)[:16, :ROWS]
         one_hot = jnp.dot(mine, hits, preferred_element_type=F32).astype(BF16)
         ours = (plane_along == t) & (group_along == rows_at) & token_lane
-        ours = jnp.where(ours, 1.0, 0.0).astype(BF16)[:GROUP_SLOTS, :ROWS]
-        spot = jnp.right_shift(block_down[:, :1], tp.bit_length() - 1) * 16 + slot_down
-        spots = lax.broadcasted_iota(jnp.int32, (ROWS, seq * 16), 1)
+        ours = jnp.where(ours, 1.0, 0.0).astype(BF16)[:16, :ROWS]
+        spot = jnp.right_shift(block_down[:, :1], tp.bit_length() - 1) * 2 * SLOTS + slot_down
+        spots = lax.broadcasted_iota(jnp.int32, (ROWS, seq * 2 * SLOTS), 1)
         to_group = jnp.concatenate(
             [
                 jnp.dot(
                     ours,
                     jnp.where(spots == spot + half * SLOTS, 1.0, 0.0).astype(BF16),
                     preferred_element_type=F32,
-                )
+                )[:GROUP_SLOTS]
                 for half in range(2)
             ],
             axis=0,
         ).astype(BF16)
-        spot = plane_down[:, :1] * GROUP_SLOTS + group_down
-        to_rows = jnp.where(
-            lax.broadcasted_iota(jnp.int32, (ROWS, tp * GROUP_SLOTS), 1) == spot, 1.0, 0.0
+        spot = plane_down[:, :1] * 2 * GROUP_SLOTS + group_down
+        spots = lax.broadcasted_iota(jnp.int32, (ROWS, tp * 2 * GROUP_SLOTS), 1)
+        to_rows = jnp.concatenate(
+            [jnp.where(spots == spot + half * GROUP_SLOTS, 1.0, 0.0) for half in range(2)], axis=0
         ).astype(BF16)
     else:
         overflow[0] = 0
@@ -244,13 +250,12 @@
     recv1[s] = send1[s]
     for load in loads:
         load.start()
+    vc[:, :, HEAD_SIZE:] = jnp.ones((GAME_COUNT, shard_len, HEAD_SIZE), BF16)
     await_all(0, recv1, seq - 1)
 
     if compact:
-        found = jnp.dot(
-            to_group, recv1[...].reshape(seq * 16, HEAD_SIZE), preferred_element_type=F32
-        )
-        found = jnp.concatenate([found[:GROUP_SLOTS], found[GROUP_SLOTS:]], axis=1).astype(BF16)
+        arrived = recv1[...].astype(F32).reshape(seq * 2 * SLOTS, HEAD_SIZE).astype(BF16)
+        found = jnp.dot(to_group, arrived, preferred_element_type=F32).astype(BF16)
     else:
         found = jnp.sum(recv1[...].astype(F32), axis=0).astype(BF16)
     send2[...] = found
@@ -260,22 +265,18 @@
     recv2[t] = found
     await_all(1, recv2, tp - 1)
     if compact:
-        embedded = jnp.dot(
-            to_rows, recv2[...].reshape(tp * GROUP_SLOTS, width), preferred_element_type=F32
-        )
+        arrived = recv2[...].astype(F32).reshape(tp * 2 * GROUP_SLOTS, HEAD_SIZE).astype(BF16)
+        embedded = jnp.dot(to_rows, arrived, preferred_element_type=F32)
+        embedded = jnp.concatenate([embedded[:ROWS], embedded[ROWS:]], axis=1)
     else:
         embedded = jnp.sum(recv2[...].astype(F32), axis=0)
 
     squares = jnp.sum(embedded * embedded, axis=-1, keepdims=True)
     normed = (embedded * gain[...].astype(F32)[None, :]).astype(BF16)
     need(0, 1, 2)
-    query_part = jnp.dot(normed, qw[...], preferred_element_type=F32)
-    key_part = jnp.dot(normed, kw[...], preferred_element_type=F32)
-    value_part = jnp.dot(normed, vw[...], preferred_element_type=F32)
-    for j in range(GROUP):
-        spread[pl.ds(j, ROWS, stride=16), :] = query_part[:, j * HEAD_SIZE : (j + 1) * HEAD_SIZE]
-    spread[pl.ds(8, ROWS, stride=16), :] = key_part
-    spread[pl.ds(9, ROWS, stride=16), :] = value_part
+    products = jnp.dot(normed, weights[...], preferred_element_type=F32)
+    for j in range(GROUP + 2):
+        spread[pl.ds(j, ROWS, stride=16), :] = products[:, j * HEAD_SIZE : (j + 1) * HEAD_SIZE]
     for j in range(10, 16):
         spread[pl.ds(j, ROWS, stride=16), :] = jnp.broadcast_to(squares, (ROWS, HEAD_SIZE))
     send3[...] = spread[...].reshape(ROWS, 16, HEAD_SIZE).astype(BF16)
@@ -299,58 +300,75 @@
     scaled = sums * inv_rms
     turned = scaled * cosine + pltpu.roll(scaled, HEAD_SIZE // 2, 1) * sine
     place = lax.broadcasted_iota(jnp.int32, (16, HEAD_SIZE), 0)
-    own = jnp.where(place < 9, turned, scaled).astype(BF16)
-    rows[s] = own
-
+    own = rounded(jnp.where(place < 9, turned, scaled))
+    own_queries, own_pair = own[:8], own[8:]
+    rows[s] = own_queries.astype(BF16)
     for peer in seq_peers:
         scatter_copy(3, rows.at[s], rows.at[s], (peer, t)).start()
     pending.append(lambda: await_sent(3, rows, seq - 1))
-    own_queries = own.astype(F32)[:8, :]
+    pair[0] = own_pair
+    twin = lax.rem(s + GAME_COUNT * CANDIDATE_MOVES, seq)
+    twin_copy = scatter_copy(7, pair.at[0], pair.at[1], (twin, t))
+    twin_copy.start()
     need(3, 4)
     await_all(3, rows, seq - 1)
 
     factor = scale * LOG2E
-    for g in range(GAME_COUNT):
+    games = range(GAME_COUNT)
+    chunks = [pl.ds(i, KEYS) for i in range(0, shard_len, KEYS)]
+    queries, peaks, tops, sums = [], [], [], []
+    for g in games:
         halves = [
-            rows[pl.ds(16 * a + 8 * g, 8)].astype(F32)[:, :8, :].reshape(64, HEAD_SIZE)
+            rows[pl.ds(16 * a + 8 * g, 8)].astype(F32).reshape(64, HEAD_SIZE)
             for a in range(NEW_TOKENS)
         ]
-        queries = jnp.concatenate(halves, axis=0).astype(BF16)
-        scores = lax.dot_general(
-            queries, kc[g], (((1,), (1,)), ((), ())), preferred_element_type=F32
-        )
-        slot = s * shard_len + lax.broadcasted_iota(jnp.int32, (1, shard_len), 1)
-        masked = jnp.where(slot < lengths[g], scores * factor, FLOOR)
-        top = jnp.maximum(jnp.max(masked, axis=-1, keepdims=True), LOWEST)
-        shifted = jnp.exp2(masked - top)
-        total = jnp.sum(shifted, axis=-1, keepdims=True)
-        summed = jnp.dot(shifted.astype(BF16), vc[g], preferred_element_type=F32)
-        lanes = lax.broadcasted_iota(jnp.int32, (128, HEAD_SIZE), 1)
-        packed = jnp.zeros((128, HEAD_SIZE), F32)
-        for i, piece in enumerate(in_three(top) + in_three(total)):
-            packed = jnp.where(lanes == i, piece, packed)
+        queries.append(jnp.concatenate(halves, axis=0).astype(BF16))
+        peaks.append(jnp.full((128, HEAD_SIZE), FLOOR, F32))
+    for chunk in chunks:
+        slot = s * shard_len + chunk.start + lax.broadcasted_iota(jnp.int32, (1, KEYS), 1)
+        for g in games:
+            part = lax.dot_general(
+                queries[g], kc[g, chunk, :], (((1,), (1,)), ((), ())), preferred_element_type=F32
+            )
+            part = jnp.where(slot < lengths[g], part, FLOOR)
+            scores[g, :, chunk] = part
+            for i in range(0, KEYS, HEAD_SIZE):
+                peaks[g] = jnp.maximum(peaks[g], part[:, i : i + HEAD_SIZE])
+    for g in games:
+        tops.append(jnp.maximum(jnp.max(peaks[g], axis=-1, keepdims=True), LOWEST))
+        sums.append(jnp.zeros((128, 2 * HEAD_SIZE), F32))
+    for chunk in chunks:
+        for g in games:
+            shifted = jnp.exp2((scores[g, :, chunk] - tops[g]) * factor).astype(BF16)
+            sums[g] += jnp.dot(shifted, vc[g, chunk, :], preferred_element_type=F32)
+    lanes = lax.broadcasted_iota(jnp.int32, (128, HEAD_SIZE), 1)
+    for g in games:
+        top = jnp.broadcast_to(tops[g] * factor, (128, HEAD_SIZE))
+        high, middle, low = in_three(jnp.where(lanes < 3, top, sums[g][:, HEAD_SIZE:]))
+        turn = jnp.where(lanes < 3, lanes, lanes - 3)
+        packed = jnp.where(turn == 0, high, jnp.where(turn == 1, middle, low))
         message = jnp.concatenate(
-            [summed.reshape(16, 8, HEAD_SIZE), packed.reshape(16, 8, HEAD_SIZE)], axis=1
+            [sums[g][:, :HEAD_SIZE].reshape(16, 8, HEAD_SIZE), packed.reshape(16, 8, HEAD_SIZE)],
+            axis=1,
         ).astype(BF16)
         for a in range(NEW_TOKENS):
             send5[pl.ds(16 * a + 8 * g, 8)] = message[8 * a : 8 * a + 8]
-
     for peer in seq_peers:
         scatter_copy(4, send5.at[peer], recv5.at[s], (peer, t)).start()
     pending.append(lambda: await_sent(4, send5, seq - 1))
     recv5[s] = send5[s]
 
-    twin = lax.rem(s, GAME_COUNT * CANDIDATE_MOVES)
-    firsts = rows[pl.ds(twin, 1)].astype(F32)[0]
-    seconds = rows[pl.ds(twin + 16, 1)].astype(F32)[0]
-    score_a = jnp.sum(own_queries * firsts[8:9, :], axis=-1, keepdims=True) * factor
-    score_b = jnp.sum(own_queries * seconds[8:9, :], axis=-1, keepdims=True) * factor
+    twin_copy.wait()
+    firsts = jnp.where(step >= 1, pair[1], own_pair)
+    seconds = own_pair
+    score_a = jnp.sum(own_queries * firsts[0:1, :], axis=-1, keepdims=True) * factor
+    score_b = jnp.sum(own_queries * seconds[0:1, :], axis=-1, keepdims=True) * factor
     score_b = jnp.where(step >= 1, score_b, FLOOR)
     fresh_top = jnp.maximum(score_a, score_b)
     fresh_a = jnp.exp2(score_a - fresh_top)
     fresh_b = jnp.exp2(score_b - fresh_top)
     fresh_total = fresh_a + fresh_b
-    fresh_sum = rounded(fresh_a) * firsts[9:10, :] + rounded(fresh_b) * seconds[9:10, :]
+    fresh_sum = rounded(fresh_a) * firsts[1:2, :] + rounded(fresh_b) * seconds[1:2, :]
     pick = lax.broadcasted_iota(jnp.int32, (HEAD_SIZE, 2 * HEAD_SIZE), 0)
     side = lax.broadcasted_iota(jnp.int32, (HEAD_SIZE, 2 * HEAD_SIZE), 1) >= HEAD_SIZE
     pick = pick - jnp.where(side, 3, 0)
@@ -370,19 +388,16 @@
     fresh_share = jnp.exp2(fresh_top - highest)
     whole = jnp.sum(shares * totals, axis=0) + fresh_share * fresh_total
     summed = jnp.sum(shares * parts[:, :8, :], axis=0) + fresh_share * fresh_sum
-    context = rounded(summed / whole)
-    send6[...] = context
-    here = pl.ds(pl.multiple_of(s * 8, 8), 8)
-    recv6[here, :] = context
-
+    recv6[s] = (summed / whole).astype(BF16)
     for peer in seq_peers:
-        scatter_copy(5, send6, recv6.at[here], (peer, t)).start()
-    pending.append(lambda: await_sent(5, recv6, (seq - 1) * 8))
+        scatter_copy(5, recv6.at[s], recv6.at[s], (peer, t)).start()
+    pending.append(lambda: await_sent(5, recv6, seq - 1))
     need(5)
-    await_all(5, recv6, (seq - 1) * 8)
-
+    await_all(5, recv6, seq - 1)
+
+    wide[...] = recv6[...].astype(F32).reshape(ROWS * 8, HEAD_SIZE)
     contexts = jnp.concatenate(
-        [recv6[pl.ds(j, ROWS, stride=8), :] for j in range(GROUP)], axis=1
+        [wide[pl.ds(j, ROWS, stride=8), :] for j in range(GROUP)], axis=1
     ).astype(BF16)
     product = jnp.dot(contexts, ow[...], preferred_element_type=F32)
     share = ROWS // 8
@@ -433,8 +448,8 @@
     )
 
     def run(compact):
-        row_message = (16, HEAD_SIZE) if compact else (ROWS, width)
-        group_message = (GROUP_SLOTS, width) if compact else (ROWS, width)
+        row_message = (2 * SLOTS, HEAD_SIZE) if compact else (ROWS, width)
+        group_message = (2 * GROUP_SLOTS, HEAD_SIZE) if compact else (ROWS, width)
         return pl.pallas_call(
             functools.partial(kernel, compact),
             out_shape=(
@@ -445,12 +460,10 @@
             out_specs=(pl.BlockSpec(memory_space=vmem), pl.BlockSpec(memory_space=smem)),
             scratch_shapes=[
                 vmem((4, emb_table.shape[0], emb_table.shape[1] // 4), BF16),
-                vmem(q_weight.shape, BF16),
-                vmem(key_matrix.shape, BF16),
-                vmem(value_matrix.shape, BF16),
+                vmem((width, q_weight.shape[1] + 2 * HEAD_SIZE), BF16),
                 vmem(o_weight.shape, BF16),
                 vmem(cache, BF16),
-                vmem(cache, BF16),
+                vmem((GAME_COUNT, key_cache.shape[1], 2 * HEAD_SIZE), BF16),
                 vmem((seq,) + row_message, BF16),
                 vmem((seq,) + row_message, BF16),
                 vmem(group_message, BF16),
@@ -458,17 +471,19 @@
                 vmem((ROWS * 16, HEAD_SIZE), F32),
                 vmem((ROWS, 16, HEAD_SIZE), BF16),
                 vmem((seq, 16, HEAD_SIZE), BF16),
-                vmem((ROWS, 16, HEAD_SIZE), BF16),
+                vmem((ROWS, 8, HEAD_SIZE), BF16),
+                vmem((2, 8, HEAD_SIZE), F32),
+                vmem((GAME_COUNT, NEW_TOKENS * CANDIDATE_MOVES * GROUP, key_cache.shape[1]), F32),
                 vmem((ROWS, 16, HEAD_SIZE), BF16),
                 vmem((seq, 16, HEAD_SIZE), BF16),
-                vmem((8, HEAD_SIZE), F32),
+                vmem((ROWS, 8, HEAD_SIZE), BF16),
                 vmem((ROWS * 8, HEAD_SIZE), F32),
                 vmem((tp, 8, HEAD_SIZE), F32),
                 vmem((tp, 8, HEAD_SIZE), F32),
                 pltpu.SemaphoreType.DMA((4,)),
                 pltpu.SemaphoreType.DMA((6,)),
-                pltpu.SemaphoreType.DMA((7,)),
-                pltpu.SemaphoreType.DMA((7,)),
+                pltpu.SemaphoreType.DMA((8,)),
+                pltpu.SemaphoreType.DMA((8,)),
             ],
             compiler_params=pltpu.CompilerParams(
                 collective_id=0 if compact else 1,

time: 50.3 us -> 48.8 us (0.970)
  Pallas kernels: 48.3 us -> 46.8 us
    pallas_call x1, Pallas kernels: 48.3 us -> 46.8 us  [run(): pl.pallas_call(functools.partial(kernel, compact), out_shape=(jax.ShapeDt...]
where the time goes in v3:
time: 48.8 us; the launch traced here: 48.6 us
  Pallas kernels  46.8 us (96%)
  local copies, waits for them, and re-layouts  1.24 us (3%)
  between operations  0.64 us (1%)
    pallas_call x1, Pallas kernels, run(): pl.pallas_call(functools.partial(kernel, compact), out_shape=(jax.ShapeDt...  46.8 us
    unnamed x1, local copies, waits for them, and re-layouts  1.24 us

profile of v3, /device:TPU:1, one launch (start us, length us, event | category | flops | bytes accessed | tf_op | source)
XLA Modules:
  0.0 48.6 jit_solution(10616402243336791628)
XLA Ops:
  0.0 46.8 %shard_map.111 = (bf16[4,256]{1,0:T(4,128)(2,1)}, s32[1]{0:T(128)}) custom-call(s32[2,2,8]{2,1,0:T(2,128)} %ids.1, s32[2]{0:T(128)} %lengths.1, bf16[256]{0:T(256)(128)(2,1)} %gain.1, f32[1,128]{1,0:T(1,128)} %constant.5.clone.rates, bf16[256,8192]{1,0:T(8,128)(2,1)} %emb.1, bf16[256,1024]{1,0:T(8,128)(2,1)} %q_weight.1, bf16[256,128]{1,0:T(8,128)(2,1)} %key_matrix.1, ...), custom_call_target="tpu_custom_call" | custom-call | tf_op jit(solution)/shard_map/pallas_call | solution.py:453
  47.4 1.2 %copy.17 = bf16[4,256]{1,0:T(4,128)(2,1)} copy(bf16[4,256]{1,0:T(4,128)(2,1)} %get-tuple-element.47) | data formatting | bytes 4096
  (1 shorter events, 0.0 us)

commit v4 on v3

--- a/solution.py
+++ b/solution.py
@@ -89,6 +89,7 @@
     scores,
     send5,
     recv5,
+    send6,
     recv6,
     wide,
     send7,
@@ -224,12 +225,12 @@
                 )
             send1[plane * (stripe // width) + j] = part.astype(BF16)
 
-    def scatter_copy(phase, source, target, device):
+    def scatter_copy(phase, source, target, device, arrival=None):
         return pltpu.make_async_remote_copy(
             src_ref=source,
             dst_ref=target,
             send_sem=send_sems.at[phase],
-            recv_sem=recv_sems.at[phase],
+            recv_sem=recv_sems.at[phase if arrival is None else arrival],
             device_id=device,
             device_id_type=MESH,
         )
@@ -388,25 +389,34 @@
     fresh_share = jnp.exp2(fresh_top - highest)
     whole = jnp.sum(shares * totals, axis=0) + fresh_share * fresh_total
     summed = jnp.sum(shares * parts[:, :8, :], axis=0) + fresh_share * fresh_sum
-    recv6[s] = (summed / whole).astype(BF16)
-    for peer in seq_peers:
-        scatter_copy(5, recv6.at[s], recv6.at[s], (peer, t)).start()
+    share = ROWS // 8
+    send6[...] = (summed / whole).astype(BF16)
+    band = 8 + lax.div(s, share)
+    pltpu.make_async_copy(send6, recv6.at[s], recv_sems.at[band]).start()
+    for peer in seq_peers[22:] + seq_peers[:22]:
+        scatter_copy(5, send6, recv6.at[s], (peer, t), band).start()
     pending.append(lambda: await_sent(5, recv6, seq - 1))
     need(5)
-    await_all(5, recv6, seq - 1)
-
-    wide[...] = recv6[...].astype(F32).reshape(ROWS * 8, HEAD_SIZE)
-    contexts = jnp.concatenate(
-        [wide[pl.ds(j, ROWS, stride=8), :] for j in range(GROUP)], axis=1
-    ).astype(BF16)
-    product = jnp.dot(contexts, ow[...], preferred_element_type=F32)
-    share = ROWS // 8
-    for z in range(8):
-        send7[z, 0:share, :] = product[z * share : (z + 1) * share, :HEAD_SIZE]
-        send7[z, share : 2 * share, :] = product[z * share : (z + 1) * share, HEAD_SIZE:]
-
-    for peer in tp_peers:
-        scatter_copy(6, send7.at[peer], recv7.at[t], (s, peer)).start()
+
+    for bands in ((0,), (1,), (2, 3), (4, 5, 6, 7)):
+        for z in bands:
+            await_all(8 + z, recv6, share)
+        first, count = bands[0] * share, len(bands) * share
+        wide[pl.ds(first * 8, count * 8), :] = (
+            recv6[pl.ds(first, count)].astype(F32).reshape(count * 8, HEAD_SIZE)
+        )
+        contexts = jnp.concatenate(
+            [wide[pl.ds(first * 8 + j, count, stride=8), :] for j in range(GROUP)], axis=1
+        ).astype(BF16)
+        product = jnp.dot(contexts, ow[...], preferred_element_type=F32)
+        for i, z in enumerate(bands):
+            send7[z, 0:share, :] = product[i * share : (i + 1) * share, :HEAD_SIZE]
+            send7[z, share : 2 * share, :] = product[i * share : (i + 1) * share, HEAD_SIZE:]
+
+            @pl.when(t != z)
+            def _(z=z):
+                scatter_copy(6, send7.at[z], recv7.at[t], (s, z)).start()
+
     pending.append(lambda: await_sent(6, send7, tp - 1))
     recv7[t] = send7[t]
     await_all(6, recv7, tp - 1)
@@ -476,6 +486,7 @@
                 vmem((GAME_COUNT, NEW_TOKENS * CANDIDATE_MOVES * GROUP, key_cache.shape[1]), F32),
                 vmem((ROWS, 16, HEAD_SIZE), BF16),
                 vmem((seq, 16, HEAD_SIZE), BF16),
+                vmem((8, HEAD_SIZE), BF16),
                 vmem((ROWS, 8, HEAD_SIZE), BF16),
                 vmem((ROWS * 8, HEAD_SIZE), F32),
                 vmem((tp, 8, HEAD_SIZE), F32),
@@ -483,7 +494,7 @@
                 pltpu.SemaphoreType.DMA((4,)),
                 pltpu.SemaphoreType.DMA((6,)),
                 pltpu.SemaphoreType.DMA((8,)),
-                pltpu.SemaphoreType.DMA((8,)),
+                pltpu.SemaphoreType.DMA((16,)),
             ],
             compiler_params=pltpu.CompilerParams(
                 collective_id=0 if compact else 1,

time: 48.8 us -> 46.6 us (0.955)
  Pallas kernels: 46.8 us -> 44.2 us
    pallas_call x1, Pallas kernels: 46.8 us -> 44.2 us  [run(): pl.pallas_call(functools.partial(kernel, compact), out_shape=(jax.ShapeDt...]
where the time goes in v4:
time: 46.6 us; the launch traced here: 46.1 us
  Pallas kernels  44.2 us (95%)
  local copies, waits for them, and re-layouts  1.24 us (3%)
  between operations  0.64 us (1%)
    pallas_call x1, Pallas kernels, run(): pl.pallas_call(functools.partial(kernel, compact), out_shape=(jax.ShapeDt...  44.2 us
    unnamed x1, local copies, waits for them, and re-layouts  1.24 us

profile of v4, /device:TPU:1, one launch (start us, length us, event | category | flops | bytes accessed | tf_op | source)
XLA Modules:
  0.0 46.1 jit_solution(2904532159153170418)
XLA Ops:
  0.0 44.2 %shard_map.111 = (bf16[4,256]{1,0:T(4,128)(2,1)}, s32[1]{0:T(128)}) custom-call(s32[2,2,8]{2,1,0:T(2,128)} %ids.1, s32[2]{0:T(128)} %lengths.1, bf16[256]{0:T(256)(128)(2,1)} %gain.1, f32[1,128]{1,0:T(1,128)} %constant.5.clone.rates, bf16[256,8192]{1,0:T(8,128)(2,1)} %emb.1, bf16[256,1024]{1,0:T(8,128)(2,1)} %q_weight.1, bf16[256,128]{1,0:T(8,128)(2,1)} %key_matrix.1, ...), custom_call_target="tpu_custom_call" | custom-call | tf_op jit(solution)/shard_map/pallas_call | solution.py:463
  44.8 1.2 %copy.17 = bf16[4,256]{1,0:T(4,128)(2,1)} copy(bf16[4,256]{1,0:T(4,128)(2,1)} %get-tuple-element.47) | data formatting | bytes 4096
  (1 shorter events, 0.0 us)

commit v5 on v4

--- a/solution.py
+++ b/solution.py
@@ -325,25 +325,26 @@
         ]
         queries.append(jnp.concatenate(halves, axis=0).astype(BF16))
         peaks.append(jnp.full((128, HEAD_SIZE), FLOOR, F32))
-    for chunk in chunks:
+    def score(g, chunk):
         slot = s * shard_len + chunk.start + lax.broadcasted_iota(jnp.int32, (1, KEYS), 1)
-        for g in games:
-            part = lax.dot_general(
-                queries[g], kc[g, chunk, :], (((1,), (1,)), ((), ())), preferred_element_type=F32
-            )
-            part = jnp.where(slot < lengths[g], part, FLOOR)
-            scores[g, :, chunk] = part
-            for i in range(0, KEYS, HEAD_SIZE):
-                peaks[g] = jnp.maximum(peaks[g], part[:, i : i + HEAD_SIZE])
-    for g in games:
+        part = lax.dot_general(
+            queries[g], kc[g, chunk, :], (((1,), (1,)), ((), ())), preferred_element_type=F32
+        )
+        part = jnp.where(slot < lengths[g], part, FLOOR)
+        scores[g, :, chunk] = part
+        for i in range(0, KEYS, HEAD_SIZE):
+            peaks[g] = jnp.maximum(peaks[g], part[:, i : i + HEAD_SIZE])
+
+    def settle(g):
         tops.append(jnp.maximum(jnp.max(peaks[g], axis=-1, keepdims=True), LOWEST))
         sums.append(jnp.zeros((128, 2 * HEAD_SIZE), F32))
-    for chunk in chunks:
-        for g in games:
-            shifted = jnp.exp2((scores[g, :, chunk] - tops[g]) * factor).astype(BF16)
-            sums[g] += jnp.dot(shifted, vc[g, chunk, :], preferred_element_type=F32)
-    lanes = lax.broadcasted_iota(jnp.int32, (128, HEAD_SIZE), 1)
-    for g in games:
+
+    def gather(g, chunk):
+        shifted = jnp.exp2((scores[g, :, chunk] - tops[g]) * factor).astype(BF16)
+        sums[g] += jnp.dot(shifted, vc[g, chunk, :], preferred_element_type=F32)
+
+    def send_parts(g):
+        lanes = lax.broadcasted_iota(jnp.int32, (128, HEAD_SIZE), 1)
         top = jnp.broadcast_to(tops[g] * factor, (128, HEAD_SIZE))
         high, middle, low = in_three(jnp.where(lanes < 3, top, sums[g][:, HEAD_SIZE:]))
         turn = jnp.where(lanes < 3, lanes, lanes - 3)
@@ -354,8 +355,31 @@
         ).astype(BF16)
         for a in range(NEW_TOKENS):
             send5[pl.ds(16 * a + 8 * g, 8)] = message[8 * a : 8 * a + 8]
-    for peer in seq_peers:
-        scatter_copy(4, send5.at[peer], recv5.at[s], (peer, t)).start()
+        half = lax.div(y, 2)
+        places = [(i, dx, dc) for i in range(2) for dx in (2, 1, 3, 0) for dc in (1, 0)]
+        for i, dx, dc in places:
+            plane = g + 2 * (half if i else 1 - half)
+            peer = (plane * 4 + lax.rem(x + dx, 4)) * 2 + lax.rem(core + dc, 2)
+
+            def start(peer=peer):
+                scatter_copy(4, send5.at[peer], recv5.at[s], (peer, t)).start()
+
+            if (i, dx, dc) == places[-1]:
+                pl.when(peer != s)(start)
+            else:
+                start()
+
+    for chunk in chunks:
+        score(0, chunk)
+    settle(0)
+    for chunk in chunks:
+        gather(0, chunk)
+        score(1, chunk)
+    send_parts(0)
+    settle(1)
+    for chunk in chunks:
+        gather(1, chunk)
+    send_parts(1)
     pending.append(lambda: await_sent(4, send5, seq - 1))
     recv5[s] = send5[s]
 
@@ -393,12 +417,13 @@
     send6[...] = (summed / whole).astype(BF16)
     band = 8 + lax.div(s, share)
     pltpu.make_async_copy(send6, recv6.at[s], recv_sems.at[band]).start()
-    for peer in seq_peers[22:] + seq_peers[:22]:
+    first_to_send = seq_peers[22:] + [moved(0, 2, 1), moved(0, 2, 0)]
+    for peer in first_to_send + [p for i, p in enumerate(seq_peers[:22]) if i not in (10, 16)]:
         scatter_copy(5, send6, recv6.at[s], (peer, t), band).start()
     pending.append(lambda: await_sent(5, recv6, seq - 1))
     need(5)
 
-    for bands in ((0,), (1,), (2, 3), (4, 5, 6, 7)):
+    for bands in ((0,), (1,), (2,), (3,), (4, 5, 6, 7)):
         for z in bands:
             await_all(8 + z, recv6, share)
         first, count = bands[0] * share, len(bands) * share

time: 46.6 us -> 46 us (0.987)
  no operation moved by 1% of the time
where the time goes in v5:
time: 46 us; the launch traced here: 45.7 us
  Pallas kernels  43.8 us (95%)
  local copies, waits for them, and re-layouts  1.24 us (3%)
  between operations  0.64 us (1%)
    pallas_call x1, Pallas kernels, run(): pl.pallas_call(functools.partial(kernel, compact), out_shape=(jax.ShapeDt...  43.8 us
    unnamed x1, local copies, waits for them, and re-layouts  1.24 us

profile of v5, /device:TPU:1, one launch (start us, length us, event | category | flops | bytes accessed | tf_op | source)
XLA Modules:
  0.0 45.7 jit_solution(6156219476109987280)
XLA Ops:
  0.0 43.8 %shard_map.111 = (bf16[4,256]{1,0:T(4,128)(2,1)}, s32[1]{0:T(128)}) custom-call(s32[2,2,8]{2,1,0:T(2,128)} %ids.1, s32[2]{0:T(128)} %lengths.1, bf16[256]{0:T(256)(128)(2,1)} %gain.1, f32[1,128]{1,0:T(1,128)} %constant.5.clone.rates, bf16[256,8192]{1,0:T(8,128)(2,1)} %emb.1, bf16[256,1024]{1,0:T(8,128)(2,1)} %q_weight.1, bf16[256,128]{1,0:T(8,128)(2,1)} %key_matrix.1, ...), custom_call_target="tpu_custom_call" | custom-call | tf_op jit(solution)/shard_map/pallas_call | solution.py:488
  44.4 1.2 %copy.17 = bf16[4,256]{1,0:T(4,128)(2,1)} copy(bf16[4,256]{1,0:T(4,128)(2,1)} %get-tuple-element.47) | data formatting | bytes 4096
  (1 shorter events, 0.0 us)
